TPU v7x, 32 devices: a whole 2x2x4 slice. The times are simulated.
32 devices in a mesh: branch: 2 (over core), member: 4 (over z), expert: 4 (over y, x).
Axes of the slice: x: 2, y: 2, z: 4, core: 2. Of those that a mesh axis runs over, the one named last changes fastest.
Arguments:
- latents: bfloat16 [2, 16, 256, 4096], P('branch', ('member', 'expert')), may hold values from -6 to 6
- routes: int32 [2, 16, 256, 2], P('branch', ('member', 'expert')), may hold values from 0 to 3, all different within a row; in each aligned block of 256 rows (0 to 255, 256 to 511, ..., all dimensions but the last counted through in order) at most 160 rows name the same one
- keep_mask: int32 [2, 16, 256, 2], P('branch', ('member', 'expert')), may hold values 0 or 1
- router: bfloat16 [4096, 4], replicated, may hold values from -0.09375 to 0.09375
- expert_in: bfloat16 [4, 4096, 1280], P('expert', None, 'branch'), may hold values from -0.09375 to 0.09375
- expert_out: bfloat16 [4, 1280, 4096], P('expert', 'branch'), may hold values from -0.15625 to 0.15625
Outputs:
- guided: bfloat16 [16, 256, 4096], P(('member', 'expert'), None, 'branch')
Inputs may be any that keep to these rules, and one draw needn't show every extreme that they name: The two experts of a token differ. Within each block of 256 tokens (the tokens of one device), no expert is named by more than 160 routes, a bound that some block reaches.
All inputs are finite; a program needn't handle non-finite values. No bound on the sum of `keep_mask` on one device may be relied on, other than what follows from the above.
Results may differ from a plain program's by a relative error of at most 0.0066.
Values may be sent and summed in bfloat16 or wider, within the bound.
A program may use at most 128 MiB of HBM per device.

v0:
```python
import jax
import jax.numpy as jnp
from jax import lax
from jax.sharding import PartitionSpec as P

TOP = 2


guidance_scale = 4.0


def partner_2(block, axis, stride):
    count = lax.axis_size(axis)
    route = []
    for low in range(count):
        high = low | 1 << stride
        if high != low and high < count:
            route += [(low, high), (high, low)]
    return lax.ppermute(block, axis, route)


def on_device(latents, routes, keep_mask, router, expert_in, expert_out):
    feat_width = latents.shape[-1]
    tokens = latents.reshape(-1, feat_width)
    tok_count = tokens.shape[0]
    experts = lax.axis_size("expert")
    branches = lax.axis_size("branch")
    capacity = 5 * tok_count * TOP // (4 * experts)
    chosen = routes.reshape(tok_count * TOP)
    kept = keep_mask.reshape(tok_count * TOP)
    expert_ids = jnp.arange(experts, dtype=jnp.int32)
    logits = jnp.dot(tokens, router, preferred_element_type=jnp.float32)
    picked = routes.reshape(tok_count, TOP)[:, :, None] == expert_ids[None, None, :]
    score = jax.nn.sigmoid(jnp.sum(jnp.where(picked, logits[:, None, :], 0.0), axis=-1))
    gates = score / jnp.sum(score, axis=1, keepdims=True)
    onehot = ((chosen[:, None] == expert_ids[None, :]) & (kept[:, None] == 1)).astype(jnp.int32)
    before = jnp.cumsum(onehot, axis=0) - onehot
    slot = jnp.sum(before * onehot, axis=1)
    position = jnp.where(kept == 1, chosen * capacity + slot, experts * capacity)
    source = jnp.repeat(tokens, TOP, axis=0)
    buffer = (
        jnp.zeros((experts * capacity, feat_width), jnp.bfloat16)
        .at[position]
        .set(source, mode="drop")
    )
    buffer = buffer.reshape(experts, capacity, feat_width)
    local_in = expert_in[0]
    local_out = expert_out[0]
    received = lax.all_to_all(buffer, "expert", split_axis=0, concat_axis=0, tiled=True)
    sources, slot_count, _ = received.shape
    flat_rows = received.reshape(sources * slot_count, feat_width)
    partner = partner_2(flat_rows, "branch", 0)
    combined = jnp.concatenate([flat_rows, partner], axis=0)
    hidden = jax.nn.gelu(
        jnp.dot(combined, local_in, preferred_element_type=jnp.float32), approximate=True
    ).astype(jnp.bfloat16)
    partial_sums = jnp.dot(hidden, local_out, preferred_element_type=jnp.float32)
    row_total = flat_rows.shape[0]
    returned_sum = partner_2(partial_sums[row_total:], "branch", 0)
    produced = (partial_sums[:row_total] + returned_sum).astype(jnp.bfloat16)
    produced = produced.reshape(sources, slot_count, feat_width)
    returned = lax.all_to_all(produced, "expert", split_axis=0, concat_axis=0, tiled=True)
    flat_back = returned.reshape(experts * capacity, feat_width)
    taken = flat_back[jnp.minimum(position, experts * capacity - 1)].astype(jnp.float32)
    scale_rows = gates.reshape(tok_count * TOP) * kept.astype(jnp.float32)
    moe = jnp.sum((taken * scale_rows[:, None]).reshape(tok_count, TOP, feat_width), axis=1).astype(
        jnp.bfloat16
    )
    half_width = feat_width // branches
    branch_index = lax.axis_index("branch")
    other = partner_2(moe, "branch", 0)
    cond_full = jnp.where(branch_index == 0, moe, other)
    uncond_full = jnp.where(branch_index == 0, other, moe)
    cond = lax.dynamic_slice_in_dim(cond_full, branch_index * half_width, half_width, 1)
    uncond = lax.dynamic_slice_in_dim(uncond_full, branch_index * half_width, half_width, 1)
    cond = cond.astype(jnp.float32)
    uncond = uncond.astype(jnp.float32)
    guided = (uncond + guidance_scale * (cond - uncond)).astype(jnp.bfloat16)
    return guided.reshape(latents.shape[1], latents.shape[2], half_width)


def solution(mesh):
    placed = (
        P("branch", ("member", "expert"), None, None),
        P("branch", ("member", "expert"), None, None),
        P("branch", ("member", "expert"), None, None),
        P(),
        P("expert", None, "branch"),
        P("expert", "branch", None),
    )
    return jax.shard_map(
        on_device,
        mesh=mesh,
        in_specs=placed,
        out_specs=P(("member", "expert"), None, "branch"),
        check_vma=False,
    )
```

profile of v0, /device:TPU:0, one launch (start us, length us, event | category | flops | bytes accessed | tf_op | source)
XLA Modules:
  0.0 263.5 jit_solution(8420257923426713532)
XLA Ops:
  0.0 0.0 copy-start
  0.0 0.7 broadcast_compare_fusion
  0.7 0.2 copy.19
  0.9 0.2 eq.90
  1.0 0.2 eq.85
  1.2 0.8 copy.21
  2.0 0.1 eq.86
  2.2 0.1 eq.81
  2.3 0.2 eq.80
  2.5 0.7 broadcast_multiply_fusion
  3.1 1.2 reduce-window.6
  4.4 0.2 slice_reduce_fusion
  4.6 0.2 reduce-window.9
  4.8 0.1 add_bitcast_fusion
  4.8 0.1 copy.20
  5.0 0.1 mul.72
  5.1 6.1 %broadcast_in_dim.31 = bf16[256,2,4096]{2,1,0:T(2,128)(2,1)} broadcast(bf16[256,4096]{1,0:T(8,128)(2,1)} %bitcast.60), dimensions={0,2} | broadcast | bytes 6291456 | tf_op jit(solution)/shard_map/broadcast_in_dim | solution.py:40
  11.2 7.3 %reshape.176 = bf16[512,4096]{1,0:T(8,128)(2,1)} reshape(bf16[256,2,4096]{2,1,0:T(2,128)(2,1)} %broadcast_in_dim.31) | data formatting | bytes 8388608 | tf_op jit(solution)/shard_map/reshape | solution.py:40
  18.5 0.0 slice-start
  18.5 10.8 %scatter_custom_fusion = bf16[640,4096]{1,0:T(8,128)(2,1)} fusion(s32[512]{0:T(512)S(1)} %bitcast.67, bf16[512,4096]{1,0:T(8,128)(2,1)} %reshape.176, bf16[]{:T(256)} %constant.19.clone.1), kind=kCustom, calls=%fused_computation.23 | custom fusion | bytes 5243392 | tf_op jit(solution)/shard_map/scatter | solution.py:44
  29.3 64.9 %all_to_all.10 = bf16[4,160,4096]{2,1,0:T(8,128)(2,1)S(1)} all-to-all(bf16[4,160,4096]{2,1,0:T(8,128)(2,1)} %bitcast.58), channel_id=1, replica_groups=mesh['branch'=2,'member'=4,'expert'=4] {'expert'}, dimensions={0} | all-to-all | bytes 10485760 | tf_op jit(solution)/shard_map/all_to_all | solution.py:49
  94.2 0.0 slice-start.2
  94.2 0.0 collective-permute-start
  94.2 8.8 %collective-permute-done = bf16[640,4096]{1,0:T(8,128)(2,1)} collective-permute-done((bf16[640,4096]{1,0:T(8,128)(2,1)S(1)}, bf16[640,4096]{1,0:T(8,128)(2,1)}, u32[]{:S(2)}, u32[]{:S(2)}) %collective-permute-start) | collective-permute-done | bytes 5242912 | tf_op jit(solution)/shard_map/ppermute | solution.py:19
  103.0 0.0 slice-done
  103.0 0.0 slice-done.1
  103.0 10.9 %fusion.19 = bf16[1280,640]{1,0:T(8,128)(2,1)S(1)} fusion(bf16[1,4096,640]{2,1,0:T(8,128)(2,1)S(1)} %bitcast.69, bf16[640,4096]{1,0:T(8,128)(2,1)} %collective-permute-done, bf16[640,4096]{1,0:T(8,128)(2,1)S(1)} %bitcast.62), kind=kOutput, calls=%fused_computation.20 | convolution fusion | flops 6739230720 | bytes 17367040 | tf_op jit(solution)/shard_map/dot_general | solution.py:55
  113.9 0.0 slice-done.2
  113.9 0.0 slice-done.3
  113.9 11.6 %fusion.5 = f32[1280,4096]{1,0:T(8,128)} fusion(bf16[1280,640]{1,0:T(8,128)(2,1)S(1)} %fusion.19, bf16[1,640,4096]{2,1,0:T(8,128)(2,1)S(1)} %bitcast.71), kind=kOutput, calls=%fused_computation.9 | convolution fusion | flops 6710886400 | bytes 27852800 | tf_op jit(solution)/shard_map/dot_general | solution.py:57
  125.6 4.7 %slice.20 = f32[640,4096]{1,0:T(8,128)S(1)} slice(f32[1280,4096]{1,0:T(8,128)} %fusion.5), slice={[640:1280], [0:4096]} | slice | bytes 20971520 | tf_op jit(solution)/shard_map/slice | solution.py:59
  130.2 0.2 collective-permute-start.1
  130.4 16.2 %collective-permute-done.1 = f32[640,4096]{1,0:T(8,128)} collective-permute-done((f32[640,4096]{1,0:T(8,128)S(1)}, f32[640,4096]{1,0:T(8,128)}, u32[]{:S(2)}, u32[]{:S(2)}) %collective-permute-start.1) | collective-permute-done | bytes 10485792 | tf_op jit(solution)/shard_map/ppermute | solution.py:19
  146.6 10.9 %fusion = bf16[640,4096]{1,0:T(8,128)(2,1)} fusion(f32[640,4096]{1,0:T(8,128)} %collective-permute-done.1, f32[1280,4096]{1,0:T(8,128)} %fusion.5), kind=kLoop, calls=%fused_computation.3 | loop fusion | flops 5242880 | bytes 26214400 | tf_op jit(solution)/shard_map/convert_element_type | solution.py:60
  157.5 5.4 %all-to-all-start.1 = ((bf16[4,160,4096]{2,1,0:T(8,128)(2,1)}), bf16[4,160,4096]{2,1,0:T(8,128)(2,1)}, u32[]{:S(2)}, u32[]{:S(2)}) async-start(bf16[4,160,4096]{2,1,0:T(8,128)(2,1)} %bitcast.59), calls=%async_computation.1 | async-start | bytes 10485760 | tf_op jit(solution)/shard_map/all_to_all | solution.py:62
  162.8 0.0 copy-done
  162.9 0.0 copy-done.1
  162.9 0.6 fusion.36
  163.5 0.0 copy-done.2
  163.6 0.0 copy-done.3
  163.6 0.1 copy.25
  163.8 58.1 %all-to-all-done.1 = bf16[4,160,4096]{2,1,0:T(8,128)(2,1)} async-done(((bf16[4,160,4096]{2,1,0:T(8,128)(2,1)}), bf16[4,160,4096]{2,1,0:T(8,128)(2,1)}, u32[]{:S(2)}, u32[]{:S(2)}) %all-to-all-start.1) | async-done | bytes 5242912 | tf_op jit(solution)/shard_map/all_to_all | solution.py:62
  221.8 11.7 %gather_fusion = bf16[512,4096]{1,0:T(8,128)(2,1)} fusion(bf16[640,4096]{1,0:T(8,128)(2,1)} %bitcast.9, s32[1024]{0:T(1024)S(1)} %pad_clamp_fusion), kind=kCustom, calls=%fused_computation | custom fusion | bytes 8390656 | tf_op jit(solution)/shard_map/gather | solution.py:64
  233.6 9.6 %reshape.163 = f32[256,2,4096]{2,1,0:T(2,128)} reshape(bf16[512,4096]{1,0:T(8,128)(2,1)} %gather_fusion) | data formatting | bytes 12582912 | tf_op jit(solution)/shard_map/convert_element_type | solution.py:64
  243.2 13.2 %multiply_reduce_fusion = bf16[256,4096]{1,0:T(8,128)(2,1)S(1)} fusion(f32[256,2,4096]{2,1,0:T(2,128)} %reshape.163, f32[256,2]{1,0:T(8,128)S(1)} %copy.25), kind=kLoop, calls=%fused_computation.8 | loop fusion | flops 3145728 | bytes 10487808 | tf_op jit(solution)/shard_map/reduce_sum | solution.py:66
  256.4 0.1 collective-permute-start.2
  256.5 4.3 %collective-permute-done.2 = bf16[256,4096]{1,0:T(8,128)(2,1)} collective-permute-done((bf16[256,4096]{1,0:T(8,128)(2,1)S(1)}, bf16[256,4096]{1,0:T(8,128)(2,1)}, u32[]{:S(2)}, u32[]{:S(2)}) %collective-permute-start.2) | collective-permute-done | bytes 2097184 | tf_op jit(solution)/shard_map/ppermute | solution.py:19
  260.8 2.7 %fusion.28 = bf16[1,256,2048]{2,1,0:T(8,128)(2,1)} fusion(bf16[256,4096]{1,0:T(8,128)(2,1)S(1)} %multiply_reduce_fusion, s32[]{:T(128)S(6)} %select_n.61, bf16[256,4096]{1,0:T(8,128)(2,1)} %collective-permute-done.2, pred[]{:T(512)S(6)} %eq.77), kind=kLoop, calls=%fused_computation.27 | loop fusion | flops 4194304 | bytes 3145733 | tf_op jit(solution)/shard_map/reshape | solution.py:79
  (14 shorter events, 0.1 us)
Async XLA Ops:
  0.0 162.9 %copy-start = (bf16[4096,4]{0,1:T(4,128)(2,1)S(1)}, bf16[4096,4]{0,1:T(4,128)(2,1)}, u32[]{:S(2)}) copy-start(bf16[4096,4]{0,1:T(4,128)(2,1)} %param.9) | copy-start | bytes 98308
  18.5 84.5 %slice-start = ((s8[5242880]{0:T(1024)(128)(4,1)}), s8[1048576]{0:T(1024)(128)(4,1)S(1)}, s32[]{:S(2)}) async-start(s8[5242880]{0:T(1024)(128)(4,1)} %bitcast.68), calls=%async_computation.2 | async-start | bytes 2097152
  29.3 73.7 %slice-start.1 = ((s8[5242880]{0:T(1024)(128)(4,1)}), s8[4194304]{0:T(1024)(128)(4,1)S(1)}, s32[]{:S(2)}) async-start(s8[5242880]{0:T(1024)(128)(4,1)} %bitcast.68), calls=%async_computation.3 | async-start | bytes 8388608
  94.2 19.7 %slice-start.2 = ((s8[5242880]{0:T(1024)(128)(4,1)}), s8[4194304]{0:T(1024)(128)(4,1)S(1)}, s32[]{:S(2)}) async-start(s8[5242880]{0:T(1024)(128)(4,1)} %bitcast.70), calls=%async_computation.4 | async-start | bytes 8388608
  94.2 19.7 %slice-start.3 = ((s8[5242880]{0:T(1024)(128)(4,1)}), s8[1048576]{0:T(1024)(128)(4,1)S(1)}, s32[]{:S(2)}) async-start(s8[5242880]{0:T(1024)(128)(4,1)} %bitcast.70), calls=%async_computation.5 | async-start | bytes 2097152
  94.2 8.8 %collective-permute-start = (bf16[640,4096]{1,0:T(8,128)(2,1)S(1)}, bf16[640,4096]{1,0:T(8,128)(2,1)}, u32[]{:S(2)}, u32[]{:S(2)}) collective-permute-start(bf16[640,4096]{1,0:T(8,128)(2,1)S(1)} %bitcast.61), channel_id=1, source_target_pairs={{0,16},{16,0},{1,17},{17,1},{2,18},{18,2},{3,19},{19,3},{4,20},{20... | collective-permute-start | bytes 15728648 | tf_op jit(solution)/shard_map/ppermute | solution.py:19
  130.2 16.4 %collective-permute-start.1 = (f32[640,4096]{1,0:T(8,128)S(1)}, f32[640,4096]{1,0:T(8,128)}, u32[]{:S(2)}, u32[]{:S(2)}) collective-permute-start(f32[640,4096]{1,0:T(8,128)S(1)} %slice.20), channel_id=1, source_target_pairs={{0,16},{16,0},{1,17},{17,1},{2,18},{18,2},{3,19},{19,3},{4,20},{20... | collective-permute-start | bytes 31457288 | tf_op jit(solution)/shard_map/ppermute | solution.py:19
  157.4 5.4 %copy-start.1 = (bf16[1,1,256,4096]{3,2,1,0:T(8,128)(2,1)S(1)}, bf16[1,1,256,4096]{3,2,1,0:T(8,128)(2,1)}, u32[]{:S(2)}) copy-start(bf16[1,1,256,4096]{3,2,1,0:T(8,128)(2,1)} %param.6) | copy-start | bytes 6291460
  157.4 6.1 %copy-start.2 = (s32[1,1,256,2]{2,3,1,0:T(2,128)S(1)}, s32[1,1,256,2]{2,3,1,0:T(2,128)}, u32[]{:S(2)}) copy-start(s32[1,1,256,2]{2,3,1,0:T(2,128)} %param.7) | copy-start | bytes 6148
  157.4 6.1 %copy-start.3 = (s32[1,1,256,2]{2,3,1,0:T(2,128)S(1)}, s32[1,1,256,2]{2,3,1,0:T(2,128)}, u32[]{:S(2)}) copy-start(s32[1,1,256,2]{2,3,1,0:T(2,128)} %param.8) | copy-start | bytes 6148
  157.5 64.4 %all-to-all-start.1 = ((bf16[4,160,4096]{2,1,0:T(8,128)(2,1)}), bf16[4,160,4096]{2,1,0:T(8,128)(2,1)}, u32[]{:S(2)}, u32[]{:S(2)}) async-start(bf16[4,160,4096]{2,1,0:T(8,128)(2,1)} %bitcast.59), calls=%async_computation.1 | async-start | bytes 10485760 | tf_op jit(solution)/shard_map/all_to_all | solution.py:62
  256.4 4.4 %collective-permute-start.2 = (bf16[256,4096]{1,0:T(8,128)(2,1)S(1)}, bf16[256,4096]{1,0:T(8,128)(2,1)}, u32[]{:S(2)}, u32[]{:S(2)}) collective-permute-start(bf16[256,4096]{1,0:T(8,128)(2,1)S(1)} %multiply_reduce_fusion), channel_id=1, source_target_pairs={{0,16},{16,0},{1,17},{17,1},{2,18},{18,2},{3,19},{19,3},{4,20},{20... | collective-permute-start | bytes 6291464 | tf_op jit(solution)/shard_map/ppermute | solution.py:19
where the time goes:
time: 264 us; the launch traced here: 263 us
  waiting for transfers between devices  87.3 us (33%)
  blocking collectives  64.9 us (25%)
  local copies, waits for them, and re-layouts  52.6 us (20%)
  other arithmetic  29.7 us (11%)
  matrix products  23.1 us (9%)
  starting transfers between devices  5.64 us (2%)
    all_to_all x1, blocking collectives, on_device(): lax.all_to_all(buffer, 'expert', split_axis=0, concat_axis=0, tiled=True)  64.9 us
    all_to_all x1, waiting for transfers between devices, on_device(): lax.all_to_all(produced, 'expert', split_axis=0, concat_axis=0, tiled=True)  58.1 us
    ppermute x3, waiting for transfers between devices, partner_2(): return lax.ppermute(block, axis, route)  29.2 us
    reduce_sum x1, other arithmetic, on_device(): jnp.sum((taken * scale_rows[:, None]).reshape(tok_count, TOP, feat_width)...  13.2 us
    gather x1, local copies, waits for them, and re-layouts, on_device(): flat_back[jnp.minimum(position, experts * capacity - 1)].astype(jnp.float32)  11.7 us
    dot_general x1, matrix products, on_device(): jnp.dot(hidden, local_out, preferred_element_type=jnp.float32)  11.6 us
    convert_element_type x1, other arithmetic, on_device(): produced = (partial_sums[:row_total] + returned_sum).astype(jnp.bfloat16)  10.9 us
    dot_general x1, matrix products, on_device(): jnp.dot(combined, local_in, preferred_element_type=jnp.float32)  10.9 us
  transfers between devices with their start and end apart: 4, of which 4 were waited for; matrix products, arithmetic and copies ran while one was open for 0% of the time, Pallas kernels for 0%

commit v1 on v0

v1 whole, which is shorter than its diff:
```python
import functools

import jax
import jax.numpy as jnp
from jax import lax
from jax.experimental import pallas as pl
from jax.experimental.pallas import tpu as pltpu
from jax.sharding import PartitionSpec as P

TOP = 2
guidance_scale = 4.0
MESH = pl.DeviceIdType.MESH
NO_SLOT = -4096.0
TILE = 256


def layer(
    experts,
    slots,
    tokens,
    routes,
    keep,
    router,
    w_in,
    w_out,
    guided,
    win,
    wout,
    meta,
    meta_in,
    meta_other,
    rows,
    rows_in,
    hid,
    mixed,
    own,
    part,
    part_in,
    weight_sem,
    meta_send,
    meta_recv,
    row_send,
    row_recv,
    hid_send,
    hid_recv,
    mo_send,
    mo_recv,
    part_send,
    part_recv,
):
    me = lax.axis_index("expert")
    branch = lax.axis_index("branch")
    other = 1 - branch
    count, width = tokens.shape
    half_units = w_in.shape[1]
    units = win.shape[1]
    half_width = guided.shape[1]
    slot_rows = rows.shape[1]

    barrier = pltpu.get_barrier_semaphore()
    for p in range(1, experts):
        pl.semaphore_signal(
            barrier, inc=1, device_id={"expert": me ^ p}, device_id_type=MESH
        )
    pl.semaphore_signal(barrier, inc=1, device_id={"branch": other}, device_id_type=MESH)
    pl.semaphore_wait(barrier, experts)

    unit_at = pl.multiple_of(branch * half_units, 128)
    mine_at = pl.multiple_of(branch * half_width, 128)
    theirs_at = pl.multiple_of(other * half_width, 128)
    in_here = pltpu.make_async_copy(
        w_in, win.at[:, pl.ds(unit_at, half_units)], weight_sem.at[0]
    )
    out_here = pltpu.make_async_copy(
        w_out.at[:, pl.ds(mine_at, half_width)],
        wout.at[pl.ds(unit_at, half_units), :],
        weight_sem.at[1],
    )
    in_there = pltpu.make_async_remote_copy(
        src_ref=w_in,
        dst_ref=win.at[:, pl.ds(unit_at, half_units)],
        send_sem=weight_sem.at[2],
        recv_sem=weight_sem.at[3],
        device_id={"branch": other},
        device_id_type=MESH,
    )
    out_there = pltpu.make_async_remote_copy(
        src_ref=w_out.at[:, pl.ds(theirs_at, half_width)],
        dst_ref=wout.at[pl.ds(unit_at, half_units), :],
        send_sem=weight_sem.at[4],
        recv_sem=weight_sem.at[5],
        device_id={"branch": other},
        device_id_type=MESH,
    )
    in_here.start()
    in_there.start()
    out_here.start()
    out_there.start()

    logits = lax.dot_general(
        router[...], tokens[...], (((1,), (1,)), ((), ())), preferred_element_type=jnp.float32
    )
    ids = lax.broadcasted_iota(jnp.int32, (experts, count), 0)
    scores, hits = [], []
    for k in range(TOP):
        hit = routes[k : k + 1, :] == ids
        picked = jnp.sum(jnp.where(hit, logits, 0.0), axis=0, keepdims=True)
        scores.append(1.0 / (1.0 + jnp.exp(-picked)))
        hits.append(jnp.logical_and(hit, keep[k : k + 1, :] == 1))
    total = scores[0] + scores[1]
    scale = jnp.where(branch == 0, guidance_scale, 1.0 - guidance_scale)
    gate = sum(jnp.where(hits[k], scale * (scores[k] / total), 0.0) for k in range(TOP))
    kept = jnp.logical_or(hits[0], hits[1])
    earlier = (
        lax.broadcasted_iota(jnp.int32, (count, count), 0)
        < lax.broadcasted_iota(jnp.int32, (count, count), 1)
    ).astype(jnp.float32)
    slot = jnp.dot(
        kept.astype(jnp.float32).astype(jnp.bfloat16),
        earlier.astype(jnp.bfloat16),
        preferred_element_type=jnp.float32,
    )
    slot = jnp.where(kept, slot, NO_SLOT)
    for e in range(experts):
        meta[e, 0:1, :] = slot[e : e + 1, :]
        meta[e, 1:2, :] = gate[e : e + 1, :]
        meta[e, 2:8, :] = jnp.zeros((6, count), jnp.float32)

    def row_copy(p):
        return pltpu.make_async_remote_copy(
            src_ref=rows.at[p],
            dst_ref=rows_in.at[p],
            send_sem=row_send.at[p],
            recv_sem=row_recv.at[p],
            device_id={"expert": me ^ p},
            device_id_type=MESH,
        )

    def meta_copy(p):
        return pltpu.make_async_remote_copy(
            src_ref=meta.at[me ^ p],
            dst_ref=meta_in.at[p],
            send_sem=meta_send.at[p],
            recv_sem=meta_recv.at[p],
            device_id={"expert": me ^ p},
            device_id_type=MESH,
        )

    def other_meta(p):
        return pltpu.make_async_remote_copy(
            src_ref=meta_in.at[p],
            dst_ref=meta_other.at[p],
            send_sem=mo_send.at[p],
            recv_sem=mo_recv.at[p],
            device_id={"branch": other},
            device_id_type=MESH,
        )

    def hid_copy(p):
        return pltpu.make_async_remote_copy(
            src_ref=hid.at[p, pl.ds(0, slot_rows)],
            dst_ref=hid.at[p, pl.ds(slot_rows, slot_rows)],
            send_sem=hid_send.at[p],
            recv_sem=hid_recv.at[p],
            device_id={"branch": other},
            device_id_type=MESH,
        )

    def part_copy(p):
        return pltpu.make_async_remote_copy(
            src_ref=part.at[lax.rem(p, slots)],
            dst_ref=part_in.at[p],
            send_sem=part_send.at[p],
            recv_sem=part_recv.at[p],
            device_id={"expert": me ^ p},
            device_id_type=MESH,
        )

    def fill(p, into, at):
        slot_of = meta[me ^ p, 0:1, :]
        place = (
            lax.broadcasted_iota(jnp.int32, (slot_rows, count), 0).astype(jnp.float32) == slot_of
        )
        place = place.astype(jnp.float32).astype(jnp.bfloat16)

        @pl.loop(0, width // (2 * TILE))
        def _(n):
            cols = pl.ds(pl.multiple_of(n * 2 * TILE, 2 * TILE), 2 * TILE)
            into[at, :, cols] = jnp.dot(
                place, tokens[:, cols], preferred_element_type=jnp.float32
            ).astype(jnp.bfloat16)

    @pl.loop(1, experts)
    def _(p):
        fill(p, rows, p)
        row_copy(p).start()
        meta_copy(p).start()

    fill(0, rows_in, 0)
    meta_in[0] = meta[me]
    in_here.wait()
    in_there.wait()
    out_here.wait()
    out_there.wait()

    def hidden(p):
        other_meta(p).start()

        @pl.loop(0, units // TILE)
        def _(n):
            cols = pl.ds(pl.multiple_of(n * TILE, TILE), TILE)
            pre = jnp.dot(rows_in[p], win[:, cols], preferred_element_type=jnp.float32)
            hid[p, 0:slot_rows, cols] = jax.nn.gelu(pre, approximate=True).astype(jnp.bfloat16)

        hid_copy(p).start()

    def mix(p):
        other_meta(p).wait()
        hid_copy(p).wait()
        here = jnp.transpose(meta_in[p])
        there = jnp.transpose(meta_other[p])
        lane = lax.broadcasted_iota(jnp.int32, (count, 2 * slot_rows), 1).astype(jnp.float32)
        weight = jnp.where(lane == here[:, 0:1], here[:, 1:2], 0.0) + jnp.where(
            lane == there[:, 0:1] + slot_rows, there[:, 1:2], 0.0
        )
        high = weight.astype(jnp.bfloat16)
        low = (weight - high.astype(jnp.float32)).astype(jnp.bfloat16)

        @pl.loop(0, units // TILE)
        def _(n):
            cols = pl.ds(pl.multiple_of(n * TILE, TILE), TILE)
            both = hid[p, :, cols]
            mixed[:, cols] = (
                jnp.dot(high, both, preferred_element_type=jnp.float32)
                + jnp.dot(low, both, preferred_element_type=jnp.float32)
            ).astype(jnp.bfloat16)

    hidden(0)
    mix(0)

    @pl.loop(0, half_width // TILE)
    def _(n):
        cols = pl.ds(pl.multiple_of(n * TILE, TILE), TILE)
        own[:, cols] = jnp.dot(mixed[...], wout[:, cols], preferred_element_type=jnp.float32)

    @pl.loop(1, experts)
    def _(p):
        meta_copy(p).wait()
        row_copy(p).wait()
        hidden(p)
        mix(p)
        if experts > slots:

            @pl.when(p > slots)
            def _():
                part_copy(p - slots).wait_send()

        @pl.loop(0, half_width // TILE)
        def _(n):
            cols = pl.ds(pl.multiple_of(n * TILE, TILE), TILE)
            part[lax.rem(p, slots), :, cols] = jnp.dot(
                mixed[...], wout[:, cols], preferred_element_type=jnp.float32
            ).astype(jnp.bfloat16)

        part_copy(p).start()

    @pl.loop(1, experts)
    def _(p):
        if experts > slots:

            @pl.when(p >= experts - slots)
            def _():
                part_copy(p).wait_send()
        else:
            part_copy(p).wait_send()
        part_copy(p).wait_recv()
        if experts > 4:
            own[...] += part_in[p].astype(jnp.float32)

    if experts > 4:
        guided[...] = own[...].astype(jnp.bfloat16)
    else:

        @pl.loop(0, half_width // TILE)
        def _(n):
            cols = pl.ds(pl.multiple_of(n * TILE, TILE), TILE)
            total = own[:, cols]
            for p in range(1, experts):
                total = total + part_in[p, :, cols].astype(jnp.float32)
            guided[:, cols] = total.astype(jnp.bfloat16)


def on_device(latents, routes, keep_mask, router, expert_in, expert_out):
    width = latents.shape[-1]
    tokens = latents.reshape(-1, width)
    count = tokens.shape[0]
    experts = lax.axis_size("expert")
    branches = lax.axis_size("branch")
    capacity = 5 * count * TOP // (4 * experts)
    slot_rows = -(-capacity // 16) * 16
    half_units = expert_in.shape[2]
    units = half_units * branches
    half_width = width // branches
    slots = min(experts, 4)
    routes = routes.reshape(count, TOP).T
    keep_mask = keep_mask.reshape(count, TOP).T
    bf16, f32 = jnp.bfloat16, jnp.float32
    vmem = pl.BlockSpec(memory_space=pltpu.VMEM)
    hbm = pl.BlockSpec(memory_space=pl.ANY)
    dma = pltpu.SemaphoreType.DMA
    guided = pl.pallas_call(
        functools.partial(layer, experts, slots),
        out_shape=jax.ShapeDtypeStruct((count, half_width), bf16),
        in_specs=[vmem, vmem, vmem, vmem, hbm, hbm],
        out_specs=vmem,
        scratch_shapes=[
            pltpu.VMEM((width, units), bf16),
            pltpu.VMEM((units, half_width), bf16),
            pltpu.VMEM((experts, 8, count), f32),
            pltpu.VMEM((experts, 8, count), f32),
            pltpu.VMEM((experts, 8, count), f32),
            pltpu.VMEM((experts, slot_rows, width), bf16),
            pltpu.VMEM((experts, slot_rows, width), bf16),
            pltpu.VMEM((experts, 2 * slot_rows, units), bf16),
            pltpu.VMEM((count, units), bf16),
            pltpu.VMEM((count, half_width), f32),
            pltpu.VMEM((slots, count, half_width), bf16),
            pltpu.VMEM((experts, count, half_width), bf16),
            dma((6,)),
        ]
        + [dma((experts,))] * 10,
        compiler_params=pltpu.CompilerParams(
            collective_id=0, has_side_effects=True, vmem_limit_bytes=63 * 2**20
        ),
        cost_estimate=pl.CostEstimate(
            flops=13_000_000_000, bytes_accessed=20_000_000, transcendentals=1_000_000
        ),
    )(tokens, routes, keep_mask, router.T, expert_in[0], expert_out[0])
    return guided.reshape(latents.shape[1], latents.shape[2], half_width)


def solution(mesh):
    placed = (
        P("branch", ("member", "expert"), None, None),
        P("branch", ("member", "expert"), None, None),
        P("branch", ("member", "expert"), None, None),
        P(),
        P("expert", None, "branch"),
        P("expert", "branch", None),
    )
    return jax.shard_map(
        on_device,
        mesh=mesh,
        in_specs=placed,
        out_specs=P(("member", "expert"), None, "branch"),
        check_vma=False,
    )
```

time: 264 us -> 128 us (0.48)
  Pallas kernels: 0 us -> 126 us
  waiting for transfers between devices: 87.3 us -> 0 us
  blocking collectives: 64.9 us -> 0 us
  local copies, waits for them, and re-layouts: 52.6 us -> 2.3 us
  other arithmetic: 29.7 us -> 0 us
  matrix products: 23.1 us -> 0 us
  starting transfers between devices: 5.64 us -> 0 us
    pallas_call x0 -> x1, Pallas kernels: none -> 126 us  [on_device(): pl.pallas_call(functools.partial(layer, experts, slots), out_shape=jax.Sh...]
    all_to_all x1 -> x0, blocking collectives: 64.9 us -> none  [on_device(): lax.all_to_all(buffer, 'expert', split_axis=0, concat_axis=0, tiled=True)]
    all_to_all x1 -> x0, waiting for transfers between devices: 58.1 us -> none  [on_device(): lax.all_to_all(produced, 'expert', split_axis=0, concat_axis=0, tiled=True)]
    ppermute x3 -> x0, waiting for transfers between devices: 29.2 us -> none  [partner_2(): return lax.ppermute(block, axis, route)]
    dot_general x3 -> x0, matrix products: 23.1 us -> none  [the longest x1 11.6 us: on_device(): jnp.dot(hidden, local_out, preferred_element_type=jnp.float32)]
    reduce_sum x4 -> x0, other arithmetic: 13.3 us -> none  [the longest x1 13.2 us: on_device(): jnp.sum((taken * scale_rows[:, None]).reshape(tok_count, TOP, feat_width)...]
    gather x1 -> x0, local copies, waits for them, and re-layouts: 11.7 us -> none  [on_device(): flat_back[jnp.minimum(position, experts * capacity - 1)].astype(jnp.float32)]
    convert_element_type x2 -> x0, other arithmetic: 10.9 us -> none  [the longest x1 10.9 us: on_device(): produced = (partial_sums[:row_total] + returned_sum).astype(jnp.bfloat16)]
  transfers between devices with their start and end apart: 4 -> 0, of which waited for: 4 -> 0; matrix products, arithmetic and copies ran while one was open for 0% -> 0% of each run, Pallas kernels for 0% -> 0%
where the time goes in v1:
time: 128 us
  Pallas kernels  126 us (98%)
  local copies, waits for them, and re-layouts  2.3 us (2%)
    pallas_call x1, Pallas kernels, on_device(): pl.pallas_call(functools.partial(layer, experts, slots), out_shape=jax.Sh...  126 us

profile of v1, /device:TPU:0, one launch (start us, length us, event | category | flops | bytes accessed | tf_op | source)
XLA Modules:
  0.0 127.9 jit_solution(956684239560275533)
XLA Ops:
  0.0 125.6 %shard_map.64 = bf16[256,2048]{1,0:T(8,128)(2,1)} custom-call(bf16[256,4096]{1,0:T(8,128)(2,1)} %bitcast.14, s32[2,256]{1,0:T(2,128)} %bitcast.16, s32[2,256]{1,0:T(2,128)} %bitcast.17, bf16[4,4096]{1,0:T(4,128)(2,1)} %bitcast.15, bf16[4096,640]{1,0:T(8,128)(2,1)} %bitcast.12, bf16[640,4096]{1,0:T(8,128)(2,1)} %bitcast.13), custom_call_target="tpu_custom_call" | custom-call | flops 12999999488 | bytes 20000000 | tf_op jit(solution)/shard_map/pallas_call | solution.py:311
  125.6 2.3 %copy.8 = bf16[1,256,2048]{2,1,0:T(8,128)(2,1)} copy(bf16[1,256,2048]{2,1,0:T(8,128)(2,1)} %bitcast.11) | data formatting | bytes 2097152

commit v2 on v1

--- a/solution.py
+++ b/solution.py
@@ -12,6 +12,38 @@
 MESH = pl.DeviceIdType.MESH
 NO_SLOT = -4096.0
 TILE = 256
+
+
+def find_slots(experts, branch, tokens, routes, keep, router, meta):
+    count = tokens.shape[0]
+    logits = lax.dot_general(
+        router[...], tokens[...], (((1,), (1,)), ((), ())), preferred_element_type=jnp.float32
+    )
+    ids = lax.broadcasted_iota(jnp.int32, (experts, count), 0)
+    scores, hits = [], []
+    for k in range(TOP):
+        hit = routes[k : k + 1, :] == ids
+        picked = jnp.sum(jnp.where(hit, logits, 0.0), axis=0, keepdims=True)
+        scores.append(1.0 / (1.0 + jnp.exp(-picked)))
+        hits.append(jnp.logical_and(hit, keep[k : k + 1, :] == 1))
+    total = scores[0] + scores[1]
+    scale = jnp.where(branch == 0, guidance_scale, 1.0 - guidance_scale)
+    gate = sum(jnp.where(hits[k], scale * (scores[k] / total), 0.0) for k in range(TOP))
+    kept = jnp.logical_or(hits[0], hits[1])
+    earlier = (
+        lax.broadcasted_iota(jnp.int32, (count, count), 0)
+        < lax.broadcasted_iota(jnp.int32, (count, count), 1)
+    ).astype(jnp.float32)
+    slot = jnp.dot(
+        kept.astype(jnp.float32).astype(jnp.bfloat16),
+        earlier.astype(jnp.bfloat16),
+        preferred_element_type=jnp.float32,
+    )
+    slot = jnp.where(kept, slot, NO_SLOT)
+    for e in range(experts):
+        meta[e, 0:1, :] = slot[e : e + 1, :]
+        meta[e, 1:2, :] = gate[e : e + 1, :]
+        meta[e, 2:8, :] = jnp.zeros((6, count), jnp.float32)
 
 
 def layer(
@@ -97,34 +129,7 @@
     out_here.start()
     out_there.start()
 
-    logits = lax.dot_general(
-        router[...], tokens[...], (((1,), (1,)), ((), ())), preferred_element_type=jnp.float32
-    )
-    ids = lax.broadcasted_iota(jnp.int32, (experts, count), 0)
-    scores, hits = [], []
-    for k in range(TOP):
-        hit = routes[k : k + 1, :] == ids
-        picked = jnp.sum(jnp.where(hit, logits, 0.0), axis=0, keepdims=True)
-        scores.append(1.0 / (1.0 + jnp.exp(-picked)))
-        hits.append(jnp.logical_and(hit, keep[k : k + 1, :] == 1))
-    total = scores[0] + scores[1]
-    scale = jnp.where(branch == 0, guidance_scale, 1.0 - guidance_scale)
-    gate = sum(jnp.where(hits[k], scale * (scores[k] / total), 0.0) for k in range(TOP))
-    kept = jnp.logical_or(hits[0], hits[1])
-    earlier = (
-        lax.broadcasted_iota(jnp.int32, (count, count), 0)
-        < lax.broadcasted_iota(jnp.int32, (count, count), 1)
-    ).astype(jnp.float32)
-    slot = jnp.dot(
-        kept.astype(jnp.float32).astype(jnp.bfloat16),
-        earlier.astype(jnp.bfloat16),
-        preferred_element_type=jnp.float32,
-    )
-    slot = jnp.where(kept, slot, NO_SLOT)
-    for e in range(experts):
-        meta[e, 0:1, :] = slot[e : e + 1, :]
-        meta[e, 1:2, :] = gate[e : e + 1, :]
-        meta[e, 2:8, :] = jnp.zeros((6, count), jnp.float32)
+    find_slots(experts, branch, tokens, routes, keep, router, meta)
 
     def row_copy(p):
         return pltpu.make_async_remote_copy(
@@ -286,6 +291,298 @@
             cols = pl.ds(pl.multiple_of(n * TILE, TILE), TILE)
             total = own[:, cols]
             for p in range(1, experts):
+                total = total + part_in[p, :, cols].astype(jnp.float32)
+            guided[:, cols] = total.astype(jnp.bfloat16)
+
+
+def layer_2x2(
+    tokens,
+    routes,
+    keep,
+    router,
+    w_in,
+    w_out,
+    guided,
+    win,
+    wout,
+    meta,
+    meta_in,
+    meta_other,
+    rows,
+    rows_in,
+    half_in,
+    hid,
+    mixed,
+    own,
+    late,
+    part,
+    part_in,
+    weight_sem,
+    half_send,
+    half_recv,
+    meta_send,
+    meta_recv,
+    row_send,
+    row_recv,
+    hid_send,
+    hid_recv,
+    mo_send,
+    mo_recv,
+    part_send,
+    part_recv,
+):
+    experts = 4
+    me = lax.axis_index("expert")
+    branch = lax.axis_index("branch")
+    other = 1 - branch
+    count, width = tokens.shape
+    half_units = w_in.shape[1]
+    units = win.shape[1]
+    half_width = guided.shape[1]
+    slot_rows = rows.shape[1]
+    half = width // 2
+    quarter = half_width // 2
+
+    barrier = pltpu.get_barrier_semaphore()
+    for p in range(1, experts):
+        pl.semaphore_signal(
+            barrier, inc=1, device_id={"expert": me ^ p}, device_id_type=MESH
+        )
+    pl.semaphore_signal(barrier, inc=1, device_id={"branch": other}, device_id_type=MESH)
+    pl.semaphore_wait(barrier, experts)
+
+    def to_expert(p, source, target, send, recv):
+        return pltpu.make_async_remote_copy(
+            src_ref=source,
+            dst_ref=target,
+            send_sem=send,
+            recv_sem=recv,
+            device_id={"expert": me ^ p},
+            device_id_type=MESH,
+        )
+
+    def to_core(source, target, send, recv):
+        return pltpu.make_async_remote_copy(
+            src_ref=source,
+            dst_ref=target,
+            send_sem=send,
+            recv_sem=recv,
+            device_id={"branch": other},
+            device_id_type=MESH,
+        )
+
+    def raw(p):
+        return to_expert(
+            p,
+            tokens.at[:, pl.ds((p - 1) * half, half)],
+            half_in.at[p - 1],
+            half_send.at[p - 1],
+            half_recv.at[p - 1],
+        )
+
+    raw(1).start()
+    raw(2).start()
+
+    unit_at = pl.multiple_of(branch * half_units, 128)
+    mine_at = pl.multiple_of(branch * half_width, 128)
+    theirs_at = pl.multiple_of(other * half_width, 128)
+    weights = [
+        pltpu.make_async_copy(w_in, win.at[:, pl.ds(unit_at, half_units)], weight_sem.at[0]),
+        to_core(w_in, win.at[:, pl.ds(unit_at, half_units)], weight_sem.at[2], weight_sem.at[3]),
+        pltpu.make_async_copy(
+            w_out.at[:, pl.ds(mine_at, half_width)],
+            wout.at[pl.ds(unit_at, half_units), :],
+            weight_sem.at[1],
+        ),
+        to_core(
+            w_out.at[:, pl.ds(theirs_at, half_width)],
+            wout.at[pl.ds(unit_at, half_units), :],
+            weight_sem.at[4],
+            weight_sem.at[5],
+        ),
+    ]
+    for copy in weights:
+        copy.start()
+
+    find_slots(experts, branch, tokens, routes, keep, router, meta)
+
+    def meta_copy(p):
+        return to_expert(p, meta, meta_in.at[p], meta_send.at[p], meta_recv.at[p])
+
+    for p in range(1, experts):
+        meta_copy(p).start()
+
+    def fill(slot_of, source, source_at, into, at, into_at):
+        place = (
+            lax.broadcasted_iota(jnp.int32, (slot_rows, count), 0).astype(jnp.float32) == slot_of
+        )
+        place = place.astype(jnp.float32).astype(jnp.bfloat16)
+
+        @pl.loop(0, half // (2 * TILE))
+        def _(n):
+            off = n * 2 * TILE
+            cols = pl.ds(pl.multiple_of(source_at + off, 2 * TILE), 2 * TILE)
+            out = pl.ds(pl.multiple_of(into_at + off, 2 * TILE), 2 * TILE)
+            into[at, :, out] = jnp.dot(
+                place, source[:, cols], preferred_element_type=jnp.float32
+            ).astype(jnp.bfloat16)
+
+    def direct(p):
+        cols = pl.ds((2 - p) * half, half)
+        return to_expert(
+            p, rows.at[p, :, cols], rows_in.at[p, :, cols], row_send.at[p], row_recv.at[p]
+        )
+
+    def forward(p):
+        cols = pl.ds((2 - p) * half, half)
+        return to_expert(
+            p, rows.at[3, :, cols], rows_in.at[3, :, cols], row_send.at[p + 2], row_recv.at[p + 2]
+        )
+
+    for p in (1, 2):
+        fill(meta[me ^ p, 0:1, :], tokens, (2 - p) * half, rows, p, (2 - p) * half)
+    for p in (1, 2):
+        raw(p).wait_send()
+        direct(p).start()
+    for h in range(2):
+        fill(meta[me, 0:1, :], tokens, h * half, rows_in, 0, h * half)
+    for p in range(1, experts):
+        meta_copy(p).wait()
+    for p in (1, 2):
+        raw(p).wait_recv()
+        q = 3 - p
+        fill(meta_in[p, me ^ q, 0:1, :], half_in.at[p - 1], 0, rows, 3, (p - 1) * half)
+        fill(meta_in[p, me, 0:1, :], half_in.at[p - 1], 0, rows_in, p, (p - 1) * half)
+    meta_in[0] = meta[...]
+
+    def other_meta(p):
+        return to_core(meta_in.at[p, me], meta_other.at[p], mo_send.at[p], mo_recv.at[p])
+
+    def hid_copy(p):
+        return to_core(
+            hid.at[p, pl.ds(0, slot_rows)],
+            hid.at[p, pl.ds(slot_rows, slot_rows)],
+            hid_send.at[p],
+            hid_recv.at[p],
+        )
+
+    for p in range(experts):
+        other_meta(p).start()
+
+    def hidden(p):
+        @pl.loop(0, units // TILE)
+        def _(n):
+            cols = pl.ds(pl.multiple_of(n * TILE, TILE), TILE)
+            pre = jnp.dot(rows_in[p], win[:, cols], preferred_element_type=jnp.float32)
+            hid[p, 0:slot_rows, cols] = jax.nn.gelu(pre, approximate=True).astype(jnp.bfloat16)
+
+        hid_copy(p).start()
+
+    def mix(p, into):
+        other_meta(p).wait()
+        here = jnp.transpose(meta_in[p, me])
+        there = jnp.transpose(meta_other[p])
+        lane = lax.broadcasted_iota(jnp.int32, (count, 2 * slot_rows), 1).astype(jnp.float32)
+        weight = jnp.where(lane == here[:, 0:1], here[:, 1:2], 0.0) + jnp.where(
+            lane == there[:, 0:1] + slot_rows, there[:, 1:2], 0.0
+        )
+        high = weight.astype(jnp.bfloat16)
+        low = (weight - high.astype(jnp.float32)).astype(jnp.bfloat16)
+        hid_copy(p).wait()
+
+        @pl.loop(0, units // TILE)
+        def _(n):
+            cols = pl.ds(pl.multiple_of(n * TILE, TILE), TILE)
+            both = hid[p, :, cols]
+            mixed[into, :, cols] = (
+                jnp.dot(high, both, preferred_element_type=jnp.float32)
+                + jnp.dot(low, both, preferred_element_type=jnp.float32)
+            ).astype(jnp.bfloat16)
+
+    def output(of, side, store):
+        @pl.loop(0, quarter // TILE)
+        def _(n):
+            at = pl.multiple_of(n * TILE, TILE)
+            cols = pl.ds(pl.multiple_of(side * quarter + at, TILE), TILE)
+            store(
+                cols,
+                pl.ds(at, TILE),
+                jnp.dot(mixed[of], wout[:, cols], preferred_element_type=jnp.float32),
+            )
+
+    def keep_own(cols, _, value):
+        own[:, cols] = value
+
+    def to_part(p):
+        def store(cols, _, value):
+            part[p, :, cols] = value.astype(jnp.bfloat16)
+
+        return store
+
+    def to_late(index):
+        def store(_, cols, value):
+            late[index, :, cols] = value
+
+        return store
+
+    def part_copy(p, side):
+        index = {(1, 0): 0, (1, 1): 1, (2, 0): 2, (2, 1): 3, (3, 0): 4, (3, 1): 5}[p, side]
+        cols = pl.ds(side * quarter, quarter)
+        return to_expert(
+            side + 1 if p == 3 else p,
+            part.at[p, :, cols],
+            part_in.at[p, :, cols],
+            part_send.at[index],
+            part_recv.at[index],
+        )
+
+    for copy in weights:
+        copy.wait()
+    hidden(0)
+    mix(0, 0)
+    for side in range(2):
+        output(0, side, keep_own)
+    forward(1).start()
+    forward(2).start()
+    for p in (1, 2):
+        direct(p).wait()
+        hidden(p)
+    for p in (1, 2):
+        mix(p, p)
+        output(p, p - 1, to_part(p))
+        part_copy(p, p - 1).start()
+    for p in (1, 2):
+        output(p, 2 - p, to_late(p - 1))
+    for p in (1, 2):
+        forward(p).wait()
+    hidden(3)
+    mix(3, 0)
+    for side in range(2):
+        output(0, side, to_part(3))
+        part_copy(3, side).start()
+    for side in range(2):
+        p = 2 - side
+        part_copy(3, side).wait()
+
+        @pl.loop(0, quarter // TILE)
+        def _(n):
+            at = pl.multiple_of(n * TILE, TILE)
+            cols = pl.ds(pl.multiple_of(side * quarter + at, TILE), TILE)
+            part[p, :, cols] = (
+                late[p - 1, :, pl.ds(at, TILE)] + part_in[3, :, cols].astype(jnp.float32)
+            ).astype(jnp.bfloat16)
+
+        part_copy(p, side).start()
+    for p in (1, 2):
+        part_copy(p, p - 1).wait()
+    for side in range(2):
+        part_copy(2 - side, side).wait()
+
+        @pl.loop(0, quarter // TILE)
+        def _(n):
+            cols = pl.ds(pl.multiple_of(side * quarter + n * TILE, TILE), TILE)
+            total = own[:, cols]
+            for p in (1, 2):
                 total = total + part_in[p, :, cols].astype(jnp.float32)
             guided[:, cols] = total.astype(jnp.bfloat16)
 
@@ -308,27 +605,48 @@
     vmem = pl.BlockSpec(memory_space=pltpu.VMEM)
     hbm = pl.BlockSpec(memory_space=pl.ANY)
     dma = pltpu.SemaphoreType.DMA
+    if experts == 4:
+        kernel = layer_2x2
+        shapes = [
+            ((width, units), bf16),
+            ((units, half_width), bf16),
+            ((experts, 8, count), f32),
+            ((experts, experts, 8, count), f32),
+            ((experts, 8, count), f32),
+            ((experts, slot_rows, width), bf16),
+            ((experts, slot_rows, width), bf16),
+            ((2, count, width // 2), bf16),
+            ((experts, 2 * slot_rows, units), bf16),
+            ((3, count, units), bf16),
+            ((count, half_width), f32),
+            ((2, count, half_width // 2), f32),
+            ((experts, count, half_width), bf16),
+            ((experts, count, half_width), bf16),
+        ]
+        semaphores = [6, 2, 2, 4, 4, 5, 5, 4, 4, 4, 4, 6, 6]
+    else:
+        kernel = functools.partial(layer, experts, slots)
+        shapes = [
+            ((width, units), bf16),
+            ((units, half_width), bf16),
+            ((experts, 8, count), f32),
+            ((experts, 8, count), f32),
+            ((experts, 8, count), f32),
+            ((experts, slot_rows, width), bf16),
+            ((experts, slot_rows, width), bf16),
+            ((experts, 2 * slot_rows, units), bf16),
+            ((count, units), bf16),
+            ((count, half_width), f32),
+            ((slots, count, half_width), bf16),
+            ((experts, count, half_width), bf16),
+        ]
+        semaphores = [6] + [experts] * 10
     guided = pl.pallas_call(
-        functools.partial(layer, experts, slots),
+        kernel,
         out_shape=jax.ShapeDtypeStruct((count, half_width), bf16),
         in_specs=[vmem, vmem, vmem, vmem, hbm, hbm],
         out_specs=vmem,
-        scratch_shapes=[
-            pltpu.VMEM((width, units), bf16),
-            pltpu.VMEM((units, half_width), bf16),
-            pltpu.VMEM((experts, 8, count), f32),
-            pltpu.VMEM((experts, 8, count), f32),
-            pltpu.VMEM((experts, 8, count), f32),
-            pltpu.VMEM((experts, slot_rows, width), bf16),
-            pltpu.VMEM((experts, slot_rows, width), bf16),
-            pltpu.VMEM((experts, 2 * slot_rows, units), bf16),
-            pltpu.VMEM((count, units), bf16),
-            pltpu.VMEM((count, half_width), f32),
-            pltpu.VMEM((slots, count, half_width), bf16),
-            pltpu.VMEM((experts, count, half_width), bf16),
-            dma((6,)),
-        ]
-        + [dma((experts,))] * 10,
+        scratch_shapes=[pltpu.VMEM(*s) for s in shapes] + [dma((s,)) for s in semaphores],
         compiler_params=pltpu.CompilerParams(
             collective_id=0, has_side_effects=True, vmem_limit_bytes=63 * 2**20
         ),

time: 128 us -> 100 us (0.78)
  Pallas kernels: 126 us -> 98 us
    pallas_call x1, Pallas kernels: 126 us -> 98 us  [on_device(): pl.pallas_call(kernel, out_shape=jax.ShapeDtypeStruct((count, half_width)...]
where the time goes in v2:
time: 100 us
  Pallas kernels  98 us (98%)
  local copies, waits for them, and re-layouts  2.3 us (2%)
    pallas_call x1, Pallas kernels, on_device(): pl.pallas_call(kernel, out_shape=jax.ShapeDtypeStruct((count, half_width)...  98 us
    unnamed x1, local copies, waits for them, and re-layouts  2.3 us

profile of v2, /device:TPU:0, one launch (start us, length us, event | category | flops | bytes accessed | tf_op | source)
XLA Modules:
  0.0 100.3 jit_solution(6557024595945927353)
XLA Ops:
  0.0 98.0 %shard_map.64 = bf16[256,2048]{1,0:T(8,128)(2,1)} custom-call(bf16[256,4096]{1,0:T(8,128)(2,1)} %bitcast.14, s32[2,256]{1,0:T(2,128)} %bitcast.16, s32[2,256]{1,0:T(2,128)} %bitcast.17, bf16[4,4096]{1,0:T(4,128)(2,1)} %bitcast.15, bf16[4096,640]{1,0:T(8,128)(2,1)} %bitcast.12, bf16[640,4096]{1,0:T(8,128)(2,1)} %bitcast.13), custom_call_target="tpu_custom_call" | custom-call | flops 12999999488 | bytes 20000000 | tf_op jit(solution)/shard_map/pallas_call | solution.py:644
  98.0 2.3 %copy.8 = bf16[1,256,2048]{2,1,0:T(8,128)(2,1)} copy(bf16[1,256,2048]{2,1,0:T(8,128)(2,1)} %bitcast.11) | data formatting | bytes 2097152

commit v3 on v2

--- a/solution.py
+++ b/solution.py
@@ -12,6 +12,7 @@
 MESH = pl.DeviceIdType.MESH
 NO_SLOT = -4096.0
 TILE = 256
+PIECES = 2
 
 
 def find_slots(experts, branch, tokens, routes, keep, router, meta):
@@ -342,6 +343,7 @@
     slot_rows = rows.shape[1]
     half = width // 2
     quarter = half_width // 2
+    span = quarter // PIECES
 
     barrier = pltpu.get_barrier_semaphore()
     for p in range(1, experts):
@@ -499,10 +501,10 @@
                 + jnp.dot(low, both, preferred_element_type=jnp.float32)
             ).astype(jnp.bfloat16)
 
-    def output(of, side, store):
-        @pl.loop(0, quarter // TILE)
-        def _(n):
-            at = pl.multiple_of(n * TILE, TILE)
+    def output(of, side, piece, store):
+        @pl.loop(0, span // TILE)
+        def _(n):
+            at = pl.multiple_of(piece * span + n * TILE, TILE)
             cols = pl.ds(pl.multiple_of(side * quarter + at, TILE), TILE)
             store(
                 cols,
@@ -525,9 +527,9 @@
 
         return store
 
-    def part_copy(p, side):
-        index = {(1, 0): 0, (1, 1): 1, (2, 0): 2, (2, 1): 3, (3, 0): 4, (3, 1): 5}[p, side]
-        cols = pl.ds(side * quarter, quarter)
+    def part_copy(p, side, piece):
+        index = (p - 1) * 2 * PIECES + side * PIECES + piece
+        cols = pl.ds(side * quarter + piece * span, span)
         return to_expert(
             side + 1 if p == 3 else p,
             part.at[p, :, cols],
@@ -539,52 +541,60 @@
     for copy in weights:
         copy.wait()
     hidden(0)
-    mix(0, 0)
-    for side in range(2):
-        output(0, side, keep_own)
     forward(1).start()
     forward(2).start()
+    mix(0, 0)
     for p in (1, 2):
         direct(p).wait()
         hidden(p)
     for p in (1, 2):
         mix(p, p)
-        output(p, p - 1, to_part(p))
-        part_copy(p, p - 1).start()
+        for c in range(PIECES):
+            output(p, p - 1, c, to_part(p))
+            part_copy(p, p - 1, c).start()
     for p in (1, 2):
-        output(p, 2 - p, to_late(p - 1))
+        for c in range(PIECES):
+            output(p, 2 - p, c, to_late(p - 1))
     for p in (1, 2):
         forward(p).wait()
     hidden(3)
-    mix(3, 0)
+    mix(3, 3)
+    for c in range(PIECES):
+        for side in range(2):
+            output(3, side, c, to_part(3))
+            part_copy(3, side, c).start()
     for side in range(2):
-        output(0, side, to_part(3))
-        part_copy(3, side).start()
-    for side in range(2):
-        p = 2 - side
-        part_copy(3, side).wait()
-
-        @pl.loop(0, quarter // TILE)
-        def _(n):
-            at = pl.multiple_of(n * TILE, TILE)
-            cols = pl.ds(pl.multiple_of(side * quarter + at, TILE), TILE)
-            part[p, :, cols] = (
-                late[p - 1, :, pl.ds(at, TILE)] + part_in[3, :, cols].astype(jnp.float32)
-            ).astype(jnp.bfloat16)
-
-        part_copy(p, side).start()
-    for p in (1, 2):
-        part_copy(p, p - 1).wait()
-    for side in range(2):
-        part_copy(2 - side, side).wait()
-
-        @pl.loop(0, quarter // TILE)
-        def _(n):
-            cols = pl.ds(pl.multiple_of(side * quarter + n * TILE, TILE), TILE)
-            total = own[:, cols]
-            for p in (1, 2):
-                total = total + part_in[p, :, cols].astype(jnp.float32)
-            guided[:, cols] = total.astype(jnp.bfloat16)
+        for c in range(PIECES):
+            output(0, side, c, keep_own)
+    for c in range(PIECES):
+        for side in range(2):
+            p = 2 - side
+            part_copy(3, side, c).wait()
+
+            @pl.loop(0, span // TILE)
+            def _(n):
+                at = pl.multiple_of(c * span + n * TILE, TILE)
+                cols = pl.ds(pl.multiple_of(side * quarter + at, TILE), TILE)
+                part[p, :, cols] = (
+                    late[p - 1, :, pl.ds(at, TILE)] + part_in[3, :, cols].astype(jnp.float32)
+                ).astype(jnp.bfloat16)
+
+            part_copy(p, side, c).start()
+    for c in range(PIECES):
+        for p in (1, 2):
+            part_copy(p, p - 1, c).wait()
+    for c in range(PIECES):
+        for side in range(2):
+            part_copy(2 - side, side, c).wait()
+
+            @pl.loop(0, span // TILE)
+            def _(n):
+                at = side * quarter + c * span + n * TILE
+                cols = pl.ds(pl.multiple_of(at, TILE), TILE)
+                total = own[:, cols]
+                for p in (1, 2):
+                    total = total + part_in[p, :, cols].astype(jnp.float32)
+                guided[:, cols] = total.astype(jnp.bfloat16)
 
 
 def on_device(latents, routes, keep_mask, router, expert_in, expert_out):
@@ -617,13 +627,13 @@
             ((experts, slot_rows, width), bf16),
             ((2, count, width // 2), bf16),
             ((experts, 2 * slot_rows, units), bf16),
-            ((3, count, units), bf16),
+            ((experts, count, units), bf16),
             ((count, half_width), f32),
             ((2, count, half_width // 2), f32),
             ((experts, count, half_width), bf16),
             ((experts, count, half_width), bf16),
         ]
-        semaphores = [6, 2, 2, 4, 4, 5, 5, 4, 4, 4, 4, 6, 6]
+        semaphores = [6, 2, 2, 4, 4, 5, 5, 4, 4, 4, 4, 6 * PIECES, 6 * PIECES]
     else:
         kernel = functools.partial(layer, experts, slots)
         shapes = [

time: 100 us -> 96.5 us (0.965)
  Pallas kernels: 98 us -> 94 us
    pallas_call x1, Pallas kernels: 98 us -> 94 us  [on_device(): pl.pallas_call(kernel, out_shape=jax.ShapeDtypeStruct((count, half_width)...]
where the time goes in v3:
time: 96.5 us; the launch traced here: 96.3 us
  Pallas kernels  94 us (97%)
  local copies, waits for them, and re-layouts  2.3 us (2%)
    pallas_call x1, Pallas kernels, on_device(): pl.pallas_call(kernel, out_shape=jax.ShapeDtypeStruct((count, half_width)...  94 us
    unnamed x1, local copies, waits for them, and re-layouts  2.3 us

profile of v3, /device:TPU:0, one launch (start us, length us, event | category | flops | bytes accessed | tf_op | source)
XLA Modules:
  0.0 96.3 jit_solution(5474811715414344967)
XLA Ops:
  0.0 94.0 %shard_map.64 = bf16[256,2048]{1,0:T(8,128)(2,1)} custom-call(bf16[256,4096]{1,0:T(8,128)(2,1)} %bitcast.14, s32[2,256]{1,0:T(2,128)} %bitcast.16, s32[2,256]{1,0:T(2,128)} %bitcast.17, bf16[4,4096]{1,0:T(4,128)(2,1)} %bitcast.15, bf16[4096,640]{1,0:T(8,128)(2,1)} %bitcast.12, bf16[640,4096]{1,0:T(8,128)(2,1)} %bitcast.13), custom_call_target="tpu_custom_call" | custom-call | flops 12999999488 | bytes 20000000 | tf_op jit(solution)/shard_map/pallas_call | solution.py:654
  94.0 2.3 %copy.8 = bf16[1,256,2048]{2,1,0:T(8,128)(2,1)} copy(bf16[1,256,2048]{2,1,0:T(8,128)(2,1)} %bitcast.11) | data formatting | bytes 2097152
